TPU v7x, 32 devices: a whole 2x2x4 slice. The times are simulated.
32 devices in a mesh: node: 4 (over x, core), seq: 8 (over z, y).
Axes of the slice: x: 2, y: 2, z: 4, core: 2. Of those that a mesh axis runs over, the one named last changes fastest.
Arguments:
- tokens: bfloat16 [4096, 2560], P(('node', 'seq')), may hold values from -6 to 6
- grad_out: bfloat16 [4096, 2560], P(('node', 'seq')), may hold values from -6 to 6
- expert_ids: int32 [4096, 6], P(('node', 'seq')), may hold values from 0 to 31, all different within a row; in each aligned block of 128 rows (0 to 127, 128 to 255, ...) at most 28 rows name the same one
- gate_weights: float32 [4096, 6], P(('node', 'seq')), may hold values from 0.1 to 1
- w_gate: bfloat16 [32, 2560, 768], P(('node', 'seq')), may hold values from -0.125 to 0.125
- w_up: bfloat16 [32, 2560, 768], P(('node', 'seq')), may hold values from -0.125 to 0.125
- w_down: bfloat16 [32, 768, 2560], P(('node', 'seq')), may hold values from -0.21875 to 0.21875
Outputs:
- grad_tokens: bfloat16 [4096, 2560], P(('node', 'seq'))
- grad_gate: bfloat16 [32, 2560, 768], P(('node', 'seq'))
- grad_up: bfloat16 [32, 2560, 768], P(('node', 'seq'))
- grad_down: bfloat16 [32, 768, 2560], P(('node', 'seq'))
Inputs may be any that keep to these rules, and one draw needn't show every extreme that they name: `expert_ids`: among the rows of one device no expert is named more than 28 times, a bound that some block reaches; the 6 experts of a token differ.
All inputs are finite; a program needn't handle non-finite values.
Results may differ from a plain program's by a relative error of at most 0.0064.
Values may be sent and summed in bfloat16 or wider, within the bound.
A program may use at most 128 MiB of HBM per device.

v0:
```python
import jax
import jax.numpy as jnp
from jax import lax
from jax.sharding import PartitionSpec as P


def expert_backward(rows_in, rows_grad, weight_gate, weight_up, weight_down):
    gate_pre = jnp.dot(rows_in, weight_gate, preferred_element_type=jnp.float32)
    up_pre = jnp.dot(rows_in, weight_up, preferred_element_type=jnp.float32)
    sigmoid_gate = jax.nn.sigmoid(gate_pre)
    activation = (gate_pre * sigmoid_gate * up_pre).astype(jnp.bfloat16)
    act_grad = jnp.dot(rows_grad, weight_down.T, preferred_element_type=jnp.float32)
    gate_grad = (act_grad * up_pre * sigmoid_gate * (1.0 + gate_pre * (1.0 - sigmoid_gate))).astype(
        jnp.bfloat16
    )
    up_grad = (act_grad * gate_pre * sigmoid_gate).astype(jnp.bfloat16)
    down_wgrad = jnp.dot(activation.T, rows_grad, preferred_element_type=jnp.float32).astype(
        jnp.bfloat16
    )
    gate_wgrad = jnp.dot(rows_in.T, gate_grad, preferred_element_type=jnp.float32).astype(
        jnp.bfloat16
    )
    up_wgrad = jnp.dot(rows_in.T, up_grad, preferred_element_type=jnp.float32).astype(jnp.bfloat16)
    input_grad = (
        jnp.dot(gate_grad, weight_gate.T, preferred_element_type=jnp.float32)
        + jnp.dot(up_grad, weight_up.T, preferred_element_type=jnp.float32)
    ).astype(jnp.bfloat16)
    return (gate_wgrad, up_wgrad, down_wgrad, input_grad)


def local(tokens, grad_out, expert_ids, gate_weights, w_gate, w_up, w_down):
    tok_rows, width = tokens.shape
    top_count = expert_ids.shape[1]
    node_count = lax.axis_size("node")
    seq_count = lax.axis_size("seq")
    expert_count = node_count * seq_count
    capacity = max(2, (7 * top_count * tok_rows + 6 * expert_count - 1) // (6 * expert_count))
    flat_ids = expert_ids.reshape(-1)
    entries = flat_ids.shape[0]
    one_hot = (flat_ids[:, None] == jnp.arange(expert_count, dtype=jnp.int32)[None, :]).astype(
        jnp.int32
    )
    slot_rank = jnp.sum(jnp.cumsum(one_hot, axis=0) * one_hot, axis=1) - 1
    slot_index = flat_ids * capacity + slot_rank
    slot_source = (
        jnp.full((expert_count * capacity,), entries, jnp.int32)
        .at[slot_index]
        .set(jnp.arange(entries, dtype=jnp.int32))
    )
    occupied = slot_source < entries
    clipped = jnp.minimum(slot_source, entries - 1)
    token_of = clipped // top_count
    slot_gate = jnp.where(occupied, gate_weights.reshape(-1)[clipped], jnp.zeros((), jnp.float32))
    rows_in = jnp.where(occupied[:, None], tokens[token_of], jnp.zeros((), jnp.bfloat16))
    rows_grad = (slot_gate[:, None] * grad_out[token_of].astype(jnp.float32)).astype(jnp.bfloat16)
    packed = jnp.stack([rows_in, rows_grad])
    arrived = lax.all_to_all(
        packed.reshape(2, expert_count, capacity, width),
        ("node", "seq"),
        split_axis=1,
        concat_axis=1,
        tiled=True,
    )
    arrived = arrived.reshape(2, expert_count * capacity, width)
    gate_wgrad, up_wgrad, down_wgrad, input_grad = expert_backward(
        arrived[0], arrived[1], w_gate[0], w_up[0], w_down[0]
    )
    returned = lax.all_to_all(
        input_grad.reshape(expert_count, capacity, width),
        ("node", "seq"),
        split_axis=0,
        concat_axis=0,
        tiled=True,
    )
    returned = returned.reshape(expert_count * capacity, width)
    pair_grad = returned[slot_index].astype(jnp.float32).reshape(tok_rows, top_count, width)
    grad_tokens = jnp.sum(pair_grad, axis=1).astype(jnp.bfloat16)
    return (grad_tokens, gate_wgrad[None], up_wgrad[None], down_wgrad[None])


def solution(mesh):
    return jax.shard_map(
        local,
        mesh=mesh,
        in_specs=(
            P(("node", "seq"), None),
            P(("node", "seq"), None),
            P(("node", "seq"), None),
            P(("node", "seq"), None),
            P(("node", "seq"), None, None),
            P(("node", "seq"), None, None),
            P(("node", "seq"), None, None),
        ),
        out_specs=(
            P(("node", "seq"), None),
            P(("node", "seq"), None, None),
            P(("node", "seq"), None, None),
            P(("node", "seq"), None, None),
        ),
        check_vma=False,
    )
```

profile of v0, /device:TPU:0, one launch (start us, length us, event | category | flops | bytes accessed | tf_op | source)
XLA Modules:
  0.0 528.7 jit_solution(13146357483622670429)
XLA Ops:
  2.7 0.8 copy.20
  3.7 1.7 reduce-window.6
  5.9 3.4 scatter_custom_fusion
  9.3 3.7 gather_fusion.1
  13.2 5.3 %gather_fusion.2 = bf16[896,2560]{1,0:T(8,128)(2,1)} fusion(bf16[128,2560]{1,0:T(8,128)(2,1)S(1)} %copy-done, s32[1024]{0:T(1024)S(1)} %get-tuple-element.13), kind=kCustom, calls=%fused_computation.2 | custom fusion | bytes 9178624 | tf_op jit(solution)/shard_map/gather | solution.py:55
  18.5 5.3 gather_fusion
  23.8 7.2 %gather.17 = bf16[1,32,28,2560]{3,2,1,0:T(8,128)(2,1)} reshape(bf16[896,2560]{1,0:T(8,128)(2,1)} %gather_fusion) | data formatting | bytes 9175040 | tf_op jit(solution)/shard_map/gather | solution.py:54
  31.0 7.8 %reshape.130 = f32[1,32,28,2560]{3,2,1,0:T(8,128)} reshape(bf16[896,2560]{1,0:T(8,128)(2,1)} %gather_fusion.2) | data formatting | bytes 13762560 | tf_op jit(solution)/shard_map/convert_element_type | solution.py:55
  38.8 5.7 %broadcast_select_fusion = bf16[1,32,28,2560]{3,2,1,0:T(8,128)(2,1)} fusion(bf16[1,32,28,2560]{3,2,1,0:T(8,128)(2,1)} %gather.17, pred[32,28]{1,0:T(8,128)(4,1)S(1)} %broadcast_in_dim.39), kind=kLoop, calls=%fused_computation.10 | loop fusion | flops 2293760 | bytes 9175936 | tf_op jit(solution)/shard_map/jit(_where)/select_n | solution.py:54
  44.6 1.7 copy-done.3
  46.3 2.9 multiply_convert_fusion
  49.1 9.1 %pad_maximum_fusion = bf16[2,32,28,2560]{3,2,1,0:T(8,128)(2,1)} fusion(bf16[1,32,28,2560]{3,2,1,0:T(8,128)(2,1)} %multiply_convert_fusion, bf16[1,32,28,2560]{3,2,1,0:T(8,128)(2,1)} %broadcast_select_fusion), kind=kLoop, calls=%fused_computation.5 | loop fusion | flops 4587520 | bytes 18350080 | tf_op jit(solution)/shard_map/stack | solution.py:56
  58.2 15.8 %copy.21 = bf16[2,32,28,2560]{3,0,2,1:T(2,128)(2,1)S(1)} copy(bf16[2,32,28,2560]{3,2,1,0:T(8,128)(2,1)} %pad_maximum_fusion) | data formatting | bytes 18350080 | tf_op jit(solution)/shard_map/stack | solution.py:56
  74.0 209.0 %all_to_all.10 = bf16[2,32,28,2560]{3,0,2,1:T(2,128)(2,1)S(1)} all-to-all(bf16[2,32,28,2560]{3,0,2,1:T(2,128)(2,1)S(1)} %copy.21), channel_id=1, replica_groups=mesh['node'=4,'seq'=8] {'node','seq'}, dimensions={1} | all-to-all | bytes 18350080 | tf_op jit(solution)/shard_map/all_to_all | solution.py:57
  283.0 41.4 %slice_reduce_fusion.1 = (bf16[32,28,2560]{2,1,0:T(8,128)(2,1)}, bf16[32,28,2560]{2,1,0:T(8,128)(2,1)}) fusion(bf16[2,32,28,2560]{3,0,2,1:T(2,128)(2,1)S(1)} %all_to_all.10), kind=kLoop, calls=%fused_computation.8 | loop fusion | bytes 18350080 | tf_op jit(solution)/shard_map/slice | solution.py:66
  324.4 7.2 %squeeze.15 = bf16[896,2560]{1,0:T(8,128)(2,1)} reshape(bf16[32,28,2560]{2,1,0:T(8,128)(2,1)} %get-tuple-element.4) | data formatting | bytes 9175040 | tf_op jit(solution)/shard_map/squeeze | solution.py:66
  331.7 7.2 %squeeze.17 = bf16[896,2560]{1,0:T(8,128)(2,1)} reshape(bf16[32,28,2560]{2,1,0:T(8,128)(2,1)} %get-tuple-element.5) | data formatting | bytes 9175040 | tf_op jit(solution)/shard_map/squeeze | solution.py:66
  338.9 6.9 %fusion.5 = f32[896,768]{1,0:T(8,128)S(1)} fusion(bf16[896,2560]{1,0:T(8,128)(2,1)} %squeeze.17, bf16[1,2560,768]{2,1,0:T(8,128)(2,1)} %param.11), kind=kOutput, calls=%fused_computation.19 | convolution fusion | flops 3523215360 | bytes 11272192 | tf_op jit(solution)/shard_map/dot_general | solution.py:8
  345.8 3.7 fusion.8
  349.6 5.4 %multiply_convert_fusion.2 = (bf16[896,768]{1,0:T(8,128)(2,1)}, bf16[896,768]{1,0:T(8,128)(2,1)S(1)}) fusion(f32[896,768]{1,0:T(8,128)S(1)} %fusion.5, f32[896,768]{1,0:T(8,128)S(1)} %fusion.8, bf16[896,2560]{1,0:T(8,128)(2,1)S(1)} %bitcast.49, bf16[1,768,2560]{2,1,0:T(8,128)(2,1)S(1)} %copy-done.5), kind=kOutput, calls=%fused_computation.27 | convolution fusion | flops 3532161024 | bytes 16777216 | tf_op jit(solution)/shard_map/dot_general | solution.py:12
  355.0 3.8 fusion.3
  358.8 6.9 %add_convert_fusion = bf16[896,2560]{1,0:T(8,128)(2,1)} fusion(f32[896,2560]{1,0:T(8,128)S(1)} %fusion.3, bf16[896,768]{1,0:T(8,128)(2,1)} %get-tuple-element.8, bf16[1,2560,768]{2,1,0:T(8,128)(2,1)S(1)} %copy-done.7), kind=kOutput, calls=%fused_computation.9 | convolution fusion | flops 3527802880 | bytes 19070976 | tf_op jit(solution)/shard_map/dot_general | solution.py:26
  365.6 7.2 %reshape.128 = bf16[32,28,2560]{2,1,0:T(8,128)(2,1)} reshape(bf16[896,2560]{1,0:T(8,128)(2,1)} %add_convert_fusion) | data formatting | bytes 9175040 | tf_op jit(solution)/shard_map/reshape | solution.py:69
  372.8 3.9 all-to-all-start.1
  376.7 9.1 %fusion.1 = bf16[1,2560,768]{2,1,0:T(8,128)(2,1)} fusion(bf16[896,2560]{1,0:T(8,128)(2,1)} %squeeze.17, bf16[896,768]{1,0:T(8,128)(2,1)} %get-tuple-element.8), kind=kOutput, calls=%fused_computation.15 | convolution fusion | flops 3525181440 | bytes 9895936 | tf_op jit(solution)/shard_map/dot_general | solution.py:23
  385.9 8.3 %fusion = bf16[1,2560,768]{2,1,0:T(8,128)(2,1)} fusion(bf16[896,2560]{1,0:T(8,128)(2,1)} %squeeze.17, bf16[896,768]{1,0:T(8,128)(2,1)S(1)} %get-tuple-element.9), kind=kOutput, calls=%fused_computation.14 | convolution fusion | flops 3525181440 | bytes 9895936 | tf_op jit(solution)/shard_map/dot_general | solution.py:20
  394.1 5.9 %fusion.2 = bf16[1,768,2560]{2,1,0:T(8,128)(2,1)} fusion(bf16[896,2560]{1,0:T(8,128)(2,1)S(1)} %bitcast.51, f32[896,768]{1,0:T(8,128)S(1)} %copy-done.11, f32[896,768]{1,0:T(8,128)S(1)} %copy-done.9), kind=kOutput, calls=%fused_computation.16 | convolution fusion | flops 3529310208 | bytes 14024704 | tf_op jit(solution)/shard_map/dot_general | solution.py:17
  400.1 95.7 %all-to-all-done.1 = bf16[32,28,2560]{2,1,0:T(8,128)(2,1)} async-done(((bf16[32,28,2560]{2,1,0:T(8,128)(2,1)}), bf16[32,28,2560]{2,1,0:T(8,128)(2,1)}, u32[]{:S(2)}, u32[]{:S(2)}) %all-to-all-start.1) | async-done | bytes 4587552 | tf_op jit(solution)/shard_map/all_to_all | solution.py:68
  495.8 7.2 %reshape.129 = bf16[896,2560]{1,0:T(8,128)(2,1)} reshape(bf16[32,28,2560]{2,1,0:T(8,128)(2,1)} %all-to-all-done.1) | data formatting | bytes 9175040 | tf_op jit(solution)/shard_map/reshape | solution.py:75
  503.0 11.3 %gather_fusion.3 = bf16[768,2560]{1,0:T(8,128)(2,1)} fusion(bf16[896,2560]{1,0:T(8,128)(2,1)} %reshape.129, s32[1024]{0:T(1024)S(1)} %pad_clamp_fusion), kind=kCustom, calls=%fused_computation.3 | custom fusion | bytes 7867392 | tf_op jit(solution)/shard_map/gather | solution.py:76
  514.3 7.4 %gather.21 = bf16[128,6,2560]{2,1,0:T(8,128)(2,1)} reshape(bf16[768,2560]{1,0:T(8,128)(2,1)} %gather_fusion.3) | data formatting | bytes 7864320 | tf_op jit(solution)/shard_map/gather | solution.py:76
  521.7 6.5 %reduce_sum.22 = bf16[128,2560]{1,0:T(8,128)(2,1)} reduce(bf16[128,6,2560]{2,1,0:T(8,128)(2,1)} %gather.21, bf16[]{:T(256)} %constant.34.clone.1), dimensions={1}, to_apply=%region_4.5 | reduce | flops 1638400 | bytes 4587522 | tf_op jit(solution)/shard_map/reduce_sum | solution.py:77
  (53 shorter events, 2.9 us)
Async XLA Ops:
  0.6 12.6 %copy-start = (bf16[128,2560]{1,0:T(8,128)(2,1)S(1)}, bf16[128,2560]{1,0:T(8,128)(2,1)}, u32[]{:S(2)}) copy-start(bf16[128,2560]{1,0:T(8,128)(2,1)} %param.8) | copy-start | bytes 1966084
  13.2 5.3 %copy-start.2 = (bf16[128,2560]{1,0:T(8,128)(2,1)S(1)}, bf16[128,2560]{1,0:T(8,128)(2,1)}, u32[]{:S(2)}) copy-start(bf16[128,2560]{1,0:T(8,128)(2,1)} %param.7) | copy-start | bytes 1966084
  38.8 7.4 %copy-start.3 = (f32[1,32,28,2560]{3,2,1,0:T(8,128)S(1)}, f32[1,32,28,2560]{3,2,1,0:T(8,128)}, u32[]{:S(2)}) copy-start(f32[1,32,28,2560]{3,2,1,0:T(8,128)} %reshape.130) | copy-start | bytes 27525124
  338.9 6.9 %copy-start.4 = (bf16[896,2560]{1,0:T(8,128)(2,1)S(1)}, bf16[896,2560]{1,0:T(8,128)(2,1)}, u32[]{:S(2)}) copy-start(bf16[896,2560]{1,0:T(8,128)(2,1)} %squeeze.17) | copy-start | bytes 13762564
  338.9 6.9 %copy-start.7 = (bf16[1,2560,768]{2,1,0:T(8,128)(2,1)S(1)}, bf16[1,2560,768]{2,1,0:T(8,128)(2,1)}, u32[]{:S(2)}) copy-start(bf16[1,2560,768]{2,1,0:T(8,128)(2,1)} %param.12) | copy-start | bytes 11796484
  338.9 10.6 %slice-start = ((s8[4587520]{0:T(1024)(128)(4,1)}), s8[4194304]{0:T(1024)(128)(4,1)S(1)}, s32[]{:S(2)}) async-start(s8[4587520]{0:T(1024)(128)(4,1)} %bitcast.48), calls=%async_computation.2 | async-start | bytes 8388608
  345.8 3.7 copy-start.8
  345.8 3.8 slice-start.1
  345.8 3.8 copy-start.5
  349.6 5.4 %copy-start.10 = (f32[896,768]{1,0:T(8,128)}, f32[896,768]{1,0:T(8,128)S(1)}, u32[]{:S(2)}) copy-start(f32[896,768]{1,0:T(8,128)S(1)} %fusion.8) | copy-start | bytes 8257540
  349.6 5.4 %copy-start.6 = (bf16[1,2560,768]{2,1,0:T(8,128)(2,1)S(1)}, bf16[1,2560,768]{2,1,0:T(8,128)(2,1)}, u32[]{:S(2)}) copy-start(bf16[1,2560,768]{2,1,0:T(8,128)(2,1)} %param.11) | copy-start | bytes 11796484
  372.8 21.3 %slice-start.2 = ((s8[4587520]{0:T(1024)(128)(4,1)}), s8[393216]{0:T(1024)(128)(4,1)S(1)}, s32[]{:S(2)}) async-start(s8[4587520]{0:T(1024)(128)(4,1)} %bitcast.50), calls=%async_computation.4 | async-start | bytes 786432
  372.8 123.0 %all-to-all-start.1 = ((bf16[32,28,2560]{2,1,0:T(8,128)(2,1)}), bf16[32,28,2560]{2,1,0:T(8,128)(2,1)}, u32[]{:S(2)}, u32[]{:S(2)}) async-start(bf16[32,28,2560]{2,1,0:T(8,128)(2,1)} %reshape.128), calls=%async_computation.1 | async-start | bytes 10485760 | tf_op jit(solution)/shard_map/all_to_all | solution.py:68
  376.7 17.4 %slice-start.3 = ((s8[4587520]{0:T(1024)(128)(4,1)}), s8[4194304]{0:T(1024)(128)(4,1)S(1)}, s32[]{:S(2)}) async-start(s8[4587520]{0:T(1024)(128)(4,1)} %bitcast.50), calls=%async_computation.5 | async-start | bytes 8388608
  385.9 8.3 %copy-start.9 = (f32[896,768]{1,0:T(8,128)S(1)}, f32[896,768]{1,0:T(8,128)}, u32[]{:S(2)}) copy-start(f32[896,768]{1,0:T(8,128)} %copy-done.8) | copy-start | bytes 8257540
  385.9 8.3 %copy-start.11 = (f32[896,768]{1,0:T(8,128)S(1)}, f32[896,768]{1,0:T(8,128)}, u32[]{:S(2)}) copy-start(f32[896,768]{1,0:T(8,128)} %copy-done.10) | copy-start | bytes 8257540
  514.3 14.0 %copy-start.1 = (bf16[128,2560]{1,0:T(8,128)(2,1)S(1)}, bf16[128,2560]{1,0:T(8,128)(2,1)}, u32[]{:S(2)}) copy-start(bf16[128,2560]{1,0:T(8,128)(2,1)} %param.8) | copy-start | bytes 1966084
where the time goes:
time: 536 us; the launch traced here: 529 us
  blocking collectives  209 us (39%)
  local copies, waits for them, and re-layouts  142 us (26%)
  waiting for transfers between devices  95.7 us (18%)
  matrix products  49.8 us (9%)
  other arithmetic  26.9 us (5%)
    all_to_all x1, blocking collectives, local(): lax.all_to_all(packed.reshape(2, expert_count, capacity, width), ('node',...  209 us
    all_to_all x1, waiting for transfers between devices, local(): lax.all_to_all(input_grad.reshape(expert_count, capacity, width), ('node'...  95.7 us
    slice x1, local copies, waits for them, and re-layouts, local(): arrived[1]  41.4 us
    gather x2, local copies, waits for them, and re-layouts, local(): returned[slot_index].astype(jnp.float32).reshape(tok_rows, top_count, width)  18.7 us
    another operation x1, local copies, waits for them, and re-layouts, local(): packed = jnp.stack([rows_in, rows_grad])  15.8 us
    gather x2, local copies, waits for them, and re-layouts, local(): tokens[token_of]  12.5 us
  transfers between devices with their start and end apart: 1, of which 1 were waited for; matrix products, arithmetic and copies ran while one was open for 4% of the time, Pallas kernels for 0%

commit v1 on v0

v1 whole, which is shorter than its diff:
```python
import functools

import jax
import jax.numpy as jnp
from jax import lax
from jax.experimental import pallas as pl
from jax.experimental.pallas import tpu as pltpu
from jax.sharding import PartitionSpec as P

BF = jnp.bfloat16
F32 = jnp.float32
MESH = pl.DeviceIdType.MESH


def dot(a, b, ca=1, cb=0):
    return lax.dot_general(a, b, (((ca,), (cb,)), ((), ())), preferred_element_type=F32)


def kernel(
    sizes,
    info, tokens, grad, wg, wu, wd,
    gt, wgo, wuo, wdo,
    xall, snd, rcv, mm, infog, scale, wgv, wuv, wdv, gp, up, ag, act, gg, ug, rrv, zrv,
    info_send, info_recv, ag_send, ag_recv, pl_send, pl_recv, rt_send, rt_recv, zr_send, zr_recv,
    x_sem, w_sem, o_sem,
):
    Z, inner, NP, S, cap, R, top, tok, C, W, FE = sizes
    T = Z * tok
    rows = NP * R
    half = rows // 2
    n = lax.axis_index("node")
    s = lax.axis_index("seq")
    z = s // inner
    y = lax.rem(s, inner)
    me = n * inner + y

    def plane_dev(p):
        return (p // inner, z * inner + lax.rem(p, inner))

    def line_dev(zz):
        return (n, zz * inner + y)

    def own(a, i):
        return xall.at[i, pl.ds(pl.multiple_of(a * tok, 16), tok)]

    loads = []
    for i in range(2 * C):
        src = (tokens if i < C else grad).at[:, (i % C) * W:(i % C + 1) * W]
        load = pltpu.make_async_copy(src, own(z, i), x_sem.at[i])
        load.start()
        loads.append(load)
    pltpu.make_async_copy(wg, wgv, w_sem.at[0]).start()
    pltpu.make_async_copy(wu, wuv, w_sem.at[1]).start()
    for c in range(C):
        pltpu.make_async_copy(wd.at[:, c * W:(c + 1) * W], wdv.at[c], w_sem.at[2]).start()
    infog[z] = info[...]

    barrier = pltpu.get_barrier_semaphore()

    @pl.loop(1, NP)
    def _(d):
        pl.semaphore_signal(barrier, inc=1, device_id=plane_dev(lax.rem(me + d, NP)), device_id_type=MESH)

    for d in range(1, Z):
        pl.semaphore_signal(barrier, inc=1, device_id=line_dev(lax.rem(z + d, Z)), device_id_type=MESH)
    pl.semaphore_wait(barrier, NP - 1 + Z - 1)

    def info_copy(d):
        return pltpu.make_async_remote_copy(
            infog.at[z], infog.at[z], info_send.at[d], info_recv.at[d],
            device_id=line_dev(lax.rem(z + d, Z)), device_id_type=MESH)

    for d in range(1, Z):
        info_copy(d).start()
    for load in loads:
        load.wait()

    def ag_copy(j, step, way):
        shard = z - step if way == 0 else z + step
        to = z + 1 if way == 0 else z - 1
        ref = own(shard, j)
        return pltpu.make_async_remote_copy(
            ref, ref, ag_send.at[j, step, way], ag_recv.at[j, step, way],
            device_id=line_dev(to), device_id_type=MESH)

    def ag_sends(step, way):
        if way == 0:
            return (z >= step) & (z < Z - 1)
        return (z <= Z - 1 - step) & (z > 0)

    def ag_arrives(step, way):
        if way == 0:
            return z - 1 >= step
        return z + 1 <= Z - 1 - step

    def ag_in(j, step, way):
        shard = z - 1 - step if way == 0 else z + 1 + step
        ref = own(shard, j)
        return pltpu.make_async_remote_copy(
            ref, ref, ag_send.at[j, step, way], ag_recv.at[j, step, way],
            device_id=line_dev(z), device_id_type=MESH)

    def peer_rows(p):
        return pl.ds(pl.multiple_of(p * R, 16), R)

    def plane_copy(src, dst, p, send, recv):
        return pltpu.make_async_remote_copy(
            src.at[peer_rows(p)], dst.at[peer_rows(me)], send, recv,
            device_id=plane_dev(p), device_id_type=MESH)

    def plane_start(src, dst, send, recv):
        @pl.loop(1, NP)
        def _(d):
            plane_copy(src, dst, lax.rem(me + d, NP), send, recv).start()

    def wait_bytes(ref, sem):
        pltpu.make_async_copy(ref, ref, sem).wait()

    others = pl.ds(0, (NP - 1) * R)

    def routing():
        for d in range(1, Z):
            info_copy(d).wait_send()
            pltpu.make_async_remote_copy(
                infog.at[z], infog.at[lax.rem(z - d + Z, Z)], info_send.at[d], info_recv.at[d],
                device_id=line_dev(z), device_id_type=MESH).wait_recv()
        p_of = lax.broadcasted_iota(jnp.int32, (NP, tok), 0)
        expert = ((p_of // inner) * S + z * inner + lax.rem(p_of, inner)).astype(F32)
        before = (lax.broadcasted_iota(jnp.int32, (tok, tok), 0)
                  < lax.broadcasted_iota(jnp.int32, (tok, tok), 1)).astype(F32).astype(BF)
        slots, gates = [], []
        for zz in range(Z):
            table = infog[zz]
            hit = jnp.zeros((NP, tok), F32)
            gate = jnp.zeros((NP, tok), F32)
            for k in range(top):
                same = table[k:k + 1, :] == expert
                hit = hit + same.astype(F32)
                gate = gate + jnp.where(same, table[8 + k:9 + k, :], 0.0)
            rank = dot(hit.astype(BF), before) + float(zz * cap)
            slots.append(jnp.where(hit > 0.0, rank, -1.0))
            gates.append(gate)
        slot = jnp.concatenate(slots, axis=1)
        gate = jnp.concatenate(gates, axis=1)
        slot_id = lax.broadcasted_iota(jnp.int32, (R, T), 0).astype(F32)
        for p in range(NP):
            pick = slot_id == slot[p:p + 1, :]
            mm[p * R:(p + 1) * R, :] = pick.astype(F32).astype(BF)
            scale[p * R:(p + 1) * R, :] = jnp.sum(
                jnp.where(pick, gate[p:p + 1, :], 0.0), axis=1, keepdims=True)

    def half_rows(h):
        return pl.ds(pl.multiple_of(h * half, 16), half)

    def gather(j):
        @pl.loop(0, 2)
        def _(h):
            picked = dot(mm[half_rows(h), :], xall[j])
            factor = jnp.where(j < C, 1.0, scale[half_rows(h), :])
            snd[j, half_rows(h), :] = (picked * factor).astype(BF)

        plane_start(snd.at[j], rcv.at[j], pl_send.at[j], pl_recv.at[j])
        rcv[j, peer_rows(me), :] = snd[j, peer_rows(me), :]

    def consume(k):
        wait_bytes(rcv.at[k, others], pl_recv.at[k])

        @pl.when(k == 0)
        def _():
            wait_bytes(wgv, w_sem.at[0])
            wait_bytes(wuv, w_sem.at[1])
            wait_bytes(wdv, w_sem.at[2])

        @pl.when(k < C)
        def _():
            @pl.loop(0, 2)
            def _(h):
                block = rcv[k, half_rows(h), :]
                gp[half_rows(h), :] += dot(block, wgv[k])
                up[half_rows(h), :] += dot(block, wuv[k])

        @pl.when(k == C - 1)
        def _():
            @pl.loop(0, rows // 32)
            def _(h):
                part = pl.ds(pl.multiple_of(h * 32, 32), 32)
                g, u = gp[part, :], up[part, :]
                sig = jax.nn.sigmoid(g)
                act[part, :] = (g * sig * u).astype(BF)
                gp[part, :] = u * sig * (1.0 + g * (1.0 - sig))
                up[part, :] = g * sig

        @pl.when(k >= C)
        def _():
            @pl.loop(0, 2)
            def _(h):
                ag[half_rows(h), :] += dot(rcv[k, half_rows(h), :], wdv[k - C], 1, 1)

    @pl.loop(0, 2 * C + Z)
    def _(i):
        for step in range(Z):
            j = i - step

            @pl.when((j >= 0) & (j < 2 * C))
            def _():
                for way in range(2):
                    if step > 0:
                        @pl.when(ag_arrives(step - 1, way))
                        def _():
                            ag_in(j, step - 1, way).wait_recv()
                    if step < Z - 1:
                        @pl.when(ag_sends(step, way))
                        def _():
                            ag_copy(j, step, way).start()

        @pl.when(i == 0)
        def _():
            gp[...] = jnp.zeros_like(gp)
            up[...] = jnp.zeros_like(up)
            ag[...] = jnp.zeros_like(ag)
            routing()

        @pl.when((i >= Z - 1) & (i < 2 * C + Z - 1))
        def _():
            gather(i - (Z - 1))

        @pl.when(i >= Z)
        def _():
            consume(i - Z)

    @pl.loop(0, rows // 32)
    def _(h):
        part = pl.ds(pl.multiple_of(h * 32, 32), 32)
        gg[part, :] = (ag[part, :] * gp[part, :]).astype(BF)
        ug[part, :] = (ag[part, :] * up[part, :]).astype(BF)

    @pl.loop(0, 2 * C)
    def _(j):
        wait_bytes(snd.at[j, others], pl_send.at[j])
        for step in range(Z - 1):
            for way in range(2):
                @pl.when(ag_sends(step, way))
                def _():
                    ag_copy(j, step, way).wait_send()

    @pl.loop(0, C)
    def _(c):
        @pl.loop(0, 2)
        def _(h):
            snd[c, half_rows(h), :] = (
                dot(gg[half_rows(h), :], wgv[c], 1, 1) + dot(ug[half_rows(h), :], wuv[c], 1, 1)
            ).astype(BF)

        plane_start(snd.at[c], rrv.at[c], rt_send.at[c], rt_recv.at[c])
        rrv[c, peer_rows(me), :] = snd[c, peer_rows(me), :]

    def line_copy(c, d):
        to = lax.rem(z + d, Z)
        return pltpu.make_async_remote_copy(
            own(to, c), zrv.at[c, d - 1], zr_send.at[c, d], zr_recv.at[c, d],
            device_id=line_dev(to), device_id_type=MESH)

    def finish(c):
        total = xall[c, pl.ds(pl.multiple_of(z * tok, 16), tok), :].astype(F32)
        for d in range(1, Z):
            line_copy(c, d).wait_recv()
            total = total + zrv[c, d - 1].astype(F32)
        gt[c] = total.astype(BF)

    @pl.loop(0, C + 1)
    def _(c):
        @pl.when(c < C)
        def _():
            wgv[c] = dot(rcv[c], gg[...], 0, 0).astype(BF)
            pltpu.make_async_copy(wgv.at[c], wgo.at[c], o_sem.at[0, c]).start()
            wuv[c] = dot(rcv[c], ug[...], 0, 0).astype(BF)
            pltpu.make_async_copy(wuv.at[c], wuo.at[c], o_sem.at[1, c]).start()
            wdv[c] = dot(act[...], rcv[c + C], 0, 0).astype(BF)
            wait_bytes(rrv.at[c, others], rt_recv.at[c])
            xall[c] = dot(mm[...], rrv[c], 0, 0).astype(BF)
            for d in range(1, Z):
                line_copy(c, d).start()

        @pl.when(c > 0)
        def _():
            finish(c - 1)

    for c in range(C):
        pltpu.make_async_copy(wdv.at[c], wdo.at[:, c * W:(c + 1) * W], o_sem.at[2, c]).start()

    @pl.loop(0, C)
    def _(c):
        wait_bytes(snd.at[c, others], rt_send.at[c])
        for d in range(1, Z):
            line_copy(c, d).wait_send()
        wait_bytes(wgv.at[c], o_sem.at[0, c])
        wait_bytes(wuv.at[c], o_sem.at[1, c])
        wait_bytes(wdv.at[c], o_sem.at[2, c])


def local(tokens, grad_out, expert_ids, gate_weights, w_gate, w_up, w_down):
    tok, width = tokens.shape
    top = expert_ids.shape[1]
    N = lax.axis_size("node")
    S = lax.axis_size("seq")
    experts = N * S
    cap = max(2, (7 * top * tok + 6 * experts - 1) // (6 * experts))
    FE = w_gate.shape[2]
    Z = 4 if S % 4 == 0 else S
    inner = S // Z
    NP = N * inner
    R = -(-Z * cap // 16) * 16
    W = 512 if width % 512 == 0 else width
    C = width // W
    rows = NP * R
    sizes = (Z, inner, NP, S, cap, R, top, tok, C, W, FE)
    info = jnp.concatenate([
        jnp.pad(expert_ids.T.astype(F32), ((0, 8 - top), (0, 0))),
        jnp.pad(gate_weights.T, ((0, 8 - top), (0, 0))),
    ])
    any_spec = pl.BlockSpec(memory_space=pl.ANY)
    vmem_spec = pl.BlockSpec(memory_space=pltpu.VMEM)
    dma = pltpu.SemaphoreType.DMA
    gt, wgo, wuo, wdo = pl.pallas_call(
        functools.partial(kernel, sizes),
        out_shape=(
            jax.ShapeDtypeStruct((C, tok, W), BF),
            jax.ShapeDtypeStruct((C, W, FE), BF),
            jax.ShapeDtypeStruct((C, W, FE), BF),
            jax.ShapeDtypeStruct((FE, width), BF),
        ),
        in_specs=[vmem_spec] + [any_spec] * 5,
        out_specs=(vmem_spec, any_spec, any_spec, any_spec),
        scratch_shapes=[
            pltpu.VMEM((2 * C, Z * tok, W), BF),
            pltpu.VMEM((2 * C, rows, W), BF),
            pltpu.VMEM((2 * C, rows, W), BF),
            pltpu.VMEM((rows, Z * tok), BF),
            pltpu.VMEM((Z, 16, tok), F32),
            pltpu.VMEM((rows, 1), F32),
            pltpu.VMEM((C, W, FE), BF),
            pltpu.VMEM((C, W, FE), BF),
            pltpu.VMEM((C, FE, W), BF),
            pltpu.VMEM((rows, FE), F32),
            pltpu.VMEM((rows, FE), F32),
            pltpu.VMEM((rows, FE), F32),
            pltpu.VMEM((rows, FE), BF),
            pltpu.VMEM((rows, FE), BF),
            pltpu.VMEM((rows, FE), BF),
            pltpu.VMEM((C, rows, W), BF),
            pltpu.VMEM((C, Z - 1, tok, W), BF),
            dma((Z,)), dma((Z,)),
            dma((2 * C, Z - 1, 2)), dma((2 * C, Z - 1, 2)),
            dma((2 * C,)), dma((2 * C,)),
            dma((C,)), dma((C,)),
            dma((C, Z)), dma((C, Z)),
            dma((2 * C,)), dma((3,)), dma((3, C)),
        ],
        compiler_params=pltpu.CompilerParams(
            collective_id=0, has_side_effects=True, vmem_limit_bytes=63 * 1024 * 1024),
        cost_estimate=pl.CostEstimate(
            flops=16 * rows * width * FE, bytes_accessed=12 * width * FE, transcendentals=rows * FE),
    )(
        info, tokens, grad_out,
        w_gate[0].reshape(C, W, FE), w_up[0].reshape(C, W, FE), w_down[0],
    )
    grad_tokens = jnp.transpose(gt, (1, 0, 2)).reshape(tok, width)
    return (
        grad_tokens,
        wgo.reshape(1, width, FE),
        wuo.reshape(1, width, FE),
        wdo[None],
    )


def solution(mesh):
    spec2 = P(("node", "seq"), None)
    spec3 = P(("node", "seq"), None, None)
    return jax.shard_map(
        local,
        mesh=mesh,
        in_specs=(spec2, spec2, spec2, spec2, spec3, spec3, spec3),
        out_specs=(spec2, spec3, spec3, spec3),
        check_vma=False,
    )
```

time: 536 us -> 216 us (0.40)
  the two profiles are of different devices: /device:TPU:0 before, /device:TPU:11 now
where the time goes in v1:
time: 216 us
  Pallas kernels  201 us (93%)
  local copies, waits for them, and re-layouts  12.4 us (6%)
    pallas_call x1, Pallas kernels, local(): pl.pallas_call(functools.partial(kernel, sizes), out_shape=(jax.ShapeDtyp...  201 us
    unnamed x8, local copies, waits for them, and re-layouts  11 us

profile of v1, /device:TPU:11, one launch (start us, length us, event | category | flops | bytes accessed | tf_op | source)
XLA Modules:
  0.0 215.7 jit_solution(1834087856921970503)
XLA Ops:
  0.6 0.7 convert_bitcast_fusion
  1.3 1.3 select_maximum_fusion.info
  2.6 200.6 %shard_map.102 = (bf16[5,128,512]{2,1,0:T(8,128)(2,1)}, bf16[5,512,768]{2,1,0:T(8,128)(2,1)}, bf16[5,512,768]{2,1,0:T(8,128)(2,1)}, bf16[768,2560]{1,0:T(8,128)(2,1)}) custom-call(f32[16,128]{1,0:T(8,128)} %select_maximum_fusion.info, bf16[128,2560]{1,0:T(8,128)(2,1)} %tokens.1, bf16[128,2560]{1,0:T(8,128)(2,1)} %grad.1, bf16[5,512,768]{2,1,0:T(8,128)(2,1)} %bitcast.17, ...), custom_call_target="tpu_custom_call" | custom-call | flops 28185722880 | bytes 23592960 | tf_op jit(solution)/shard_map/pallas_call | solution.py:324
  203.3 1.4 copy.11
  204.7 1.1 copy.12
  205.8 0.0 copy-start.1
  205.8 4.4 %copy.16 = bf16[1,2560,768]{2,1,0:T(8,128)(2,1)} copy(bf16[1,2560,768]{2,1,0:T(8,128)(2,1)} %bitcast.13) | data formatting | bytes 7864320
  210.2 0.0 copy-done.1
  210.2 0.0 copy-start
  210.2 2.0 copy.17
  212.2 1.5 copy-done
  213.7 1.9 copy.18
Async XLA Ops:
  205.8 4.4 %copy-start.1 = (bf16[5,512,768]{2,1,0:T(8,128)(2,1)S(1)}, bf16[5,512,768]{2,1,0:T(8,128)(2,1)}, u32[]{:S(2)}) copy-start(bf16[5,512,768]{2,1,0:T(8,128)(2,1)} %get-tuple-element.10) | copy-start | bytes 11796484
  210.2 3.5 %copy-start = (bf16[768,2560]{1,0:T(8,128)(2,1)S(1)}, bf16[768,2560]{1,0:T(8,128)(2,1)}, u32[]{:S(2)}) copy-start(bf16[768,2560]{1,0:T(8,128)(2,1)} %get-tuple-element.11) | copy-start | bytes 11796484

commit v2 on v1

--- a/solution.py
+++ b/solution.py
@@ -19,10 +19,10 @@
 def kernel(
     sizes,
     info, tokens, grad, wg, wu, wd,
-    gt, wgo, wuo, wdo,
-    xall, snd, rcv, mm, infog, scale, wgv, wuv, wdv, gp, up, ag, act, gg, ug, rrv, zrv,
+    gt, wgv, wuv, wdv,
+    xall, snd, rcv, mm, infog, scale, gp, up, ag, act, gg, ug, rrv, zrv, rly,
     info_send, info_recv, ag_send, ag_recv, pl_send, pl_recv, rt_send, rt_recv, zr_send, zr_recv,
-    x_sem, w_sem, o_sem,
+    ry_recv, x_sem, w_sem,
 ):
     Z, inner, NP, S, cap, R, top, tok, C, W, FE = sizes
     T = Z * tok
@@ -40,6 +40,9 @@
     def line_dev(zz):
         return (n, zz * inner + y)
 
+    def cols(c):
+        return pl.ds(pl.multiple_of(c * W, 128), W)
+
     def own(a, i):
         return xall.at[i, pl.ds(pl.multiple_of(a * tok, 16), tok)]
 
@@ -51,8 +54,7 @@
         loads.append(load)
     pltpu.make_async_copy(wg, wgv, w_sem.at[0]).start()
     pltpu.make_async_copy(wu, wuv, w_sem.at[1]).start()
-    for c in range(C):
-        pltpu.make_async_copy(wd.at[:, c * W:(c + 1) * W], wdv.at[c], w_sem.at[2]).start()
+    pltpu.make_async_copy(wd, wdv, w_sem.at[2]).start()
     infog[z] = info[...]
 
     barrier = pltpu.get_barrier_semaphore()
@@ -171,7 +173,15 @@
             wait_bytes(wuv, w_sem.at[1])
             wait_bytes(wdv, w_sem.at[2])
 
-        @pl.when(k < C)
+        @pl.when(k == 0)
+        def _():
+            @pl.loop(0, 2)
+            def _(h):
+                block = rcv[k, half_rows(h), :]
+                gp[half_rows(h), :] = dot(block, wgv[k])
+                up[half_rows(h), :] = dot(block, wuv[k])
+
+        @pl.when((k > 0) & (k < C))
         def _():
             @pl.loop(0, 2)
             def _(h):
@@ -190,11 +200,17 @@
                 gp[part, :] = u * sig * (1.0 + g * (1.0 - sig))
                 up[part, :] = g * sig
 
-        @pl.when(k >= C)
+        @pl.when(k == C)
         def _():
             @pl.loop(0, 2)
             def _(h):
-                ag[half_rows(h), :] += dot(rcv[k, half_rows(h), :], wdv[k - C], 1, 1)
+                ag[half_rows(h), :] = dot(rcv[k, half_rows(h), :], wdv[:, cols(k - C)], 1, 1)
+
+        @pl.when(k > C)
+        def _():
+            @pl.loop(0, 2)
+            def _(h):
+                ag[half_rows(h), :] += dot(rcv[k, half_rows(h), :], wdv[:, cols(k - C)], 1, 1)
 
     @pl.loop(0, 2 * C + Z)
     def _(i):
@@ -215,9 +231,6 @@
 
         @pl.when(i == 0)
         def _():
-            gp[...] = jnp.zeros_like(gp)
-            up[...] = jnp.zeros_like(up)
-            ag[...] = jnp.zeros_like(ag)
             routing()
 
         @pl.when((i >= Z - 1) & (i < 2 * C + Z - 1))
@@ -254,48 +267,89 @@
         plane_start(snd.at[c], rrv.at[c], rt_send.at[c], rt_recv.at[c])
         rrv[c, peer_rows(me), :] = snd[c, peer_rows(me), :]
 
+    merge = Z == 4
+
     def line_copy(c, d):
         to = lax.rem(z + d, Z)
         return pltpu.make_async_remote_copy(
             own(to, c), zrv.at[c, d - 1], zr_send.at[c, d], zr_recv.at[c, d],
             device_id=line_dev(to), device_id_type=MESH)
+
+    def relay_copy(c, d):
+        return pltpu.make_async_remote_copy(
+            own(lax.rem(z + d, Z), c), rly.at[c], zr_send.at[c, d], ry_recv.at[c],
+            device_id=line_dev(z - 1 if d == 1 else z + 1), device_id_type=MESH)
+
+    last = Z - 1
+    middle = (z > 0) & (z < last)
+
+    def send_partials(c):
+        if merge:
+            for d, end in ((1, last), (last, 0)):
+                @pl.when(z == end)
+                def _():
+                    relay_copy(c, d).start()
+
+            for d, end in ((1, last), (last, 0)):
+                @pl.when(z != end)
+                def _():
+                    line_copy(c, d).start()
+
+            @pl.when(~middle)
+            def _():
+                line_copy(c, 2).start()
+        else:
+            for d in range(1, Z):
+                line_copy(c, d).start()
+
+    def pass_on(c):
+        if merge:
+            @pl.when(middle)
+            def _():
+                relay_copy(c, 1).wait_recv()
+                mine = pl.ds(pl.multiple_of(lax.rem(z + 2, Z) * tok, 16), tok)
+                xall[c, mine, :] = (xall[c, mine, :].astype(F32) + rly[c].astype(F32)).astype(BF)
+                line_copy(c, 2).start()
 
     def finish(c):
         total = xall[c, pl.ds(pl.multiple_of(z * tok, 16), tok), :].astype(F32)
         for d in range(1, Z):
-            line_copy(c, d).wait_recv()
-            total = total + zrv[c, d - 1].astype(F32)
-        gt[c] = total.astype(BF)
-
-    @pl.loop(0, C + 1)
+            none = 0 if d == 1 else last
+            if merge and d != 2:
+                @pl.when(z != none)
+                def _():
+                    line_copy(c, d).wait_recv()
+
+                total = total + jnp.where(z != none, zrv[c, d - 1].astype(F32), 0.0)
+            else:
+                line_copy(c, d).wait_recv()
+                total = total + zrv[c, d - 1].astype(F32)
+        gt[:, cols(c)] = total.astype(BF)
+
+    @pl.loop(0, C + 2)
     def _(c):
         @pl.when(c < C)
         def _():
             wgv[c] = dot(rcv[c], gg[...], 0, 0).astype(BF)
-            pltpu.make_async_copy(wgv.at[c], wgo.at[c], o_sem.at[0, c]).start()
             wuv[c] = dot(rcv[c], ug[...], 0, 0).astype(BF)
-            pltpu.make_async_copy(wuv.at[c], wuo.at[c], o_sem.at[1, c]).start()
-            wdv[c] = dot(act[...], rcv[c + C], 0, 0).astype(BF)
+            wdv[:, cols(c)] = dot(act[...], rcv[c + C], 0, 0).astype(BF)
             wait_bytes(rrv.at[c, others], rt_recv.at[c])
             xall[c] = dot(mm[...], rrv[c], 0, 0).astype(BF)
-            for d in range(1, Z):
-                line_copy(c, d).start()
-
-        @pl.when(c > 0)
-        def _():
-            finish(c - 1)
-
-    for c in range(C):
-        pltpu.make_async_copy(wdv.at[c], wdo.at[:, c * W:(c + 1) * W], o_sem.at[2, c]).start()
+            send_partials(c)
+
+        @pl.when((c > 0) & (c < C + 1))
+        def _():
+            pass_on(c - 1)
+
+        @pl.when(c > 1)
+        def _():
+            finish(c - 2)
 
     @pl.loop(0, C)
     def _(c):
         wait_bytes(snd.at[c, others], rt_send.at[c])
         for d in range(1, Z):
             line_copy(c, d).wait_send()
-        wait_bytes(wgv.at[c], o_sem.at[0, c])
-        wait_bytes(wuv.at[c], o_sem.at[1, c])
-        wait_bytes(wdv.at[c], o_sem.at[2, c])
 
 
 def local(tokens, grad_out, expert_ids, gate_weights, w_gate, w_up, w_down):
@@ -310,7 +364,7 @@
     inner = S // Z
     NP = N * inner
     R = -(-Z * cap // 16) * 16
-    W = 512 if width % 512 == 0 else width
+    W = 256 if width % 256 == 0 else width
     C = width // W
     rows = NP * R
     sizes = (Z, inner, NP, S, cap, R, top, tok, C, W, FE)
@@ -324,13 +378,13 @@
     gt, wgo, wuo, wdo = pl.pallas_call(
         functools.partial(kernel, sizes),
         out_shape=(
-            jax.ShapeDtypeStruct((C, tok, W), BF),
-            jax.ShapeDtypeStruct((C, W, FE), BF),
-            jax.ShapeDtypeStruct((C, W, FE), BF),
-            jax.ShapeDtypeStruct((FE, width), BF),
+            pltpu.VMEM((tok, width), BF),
+            pltpu.VMEM((C, W, FE), BF),
+            pltpu.VMEM((C, W, FE), BF),
+            pltpu.VMEM((FE, width), BF),
         ),
         in_specs=[vmem_spec] + [any_spec] * 5,
-        out_specs=(vmem_spec, any_spec, any_spec, any_spec),
+        out_specs=(vmem_spec,) * 4,
         scratch_shapes=[
             pltpu.VMEM((2 * C, Z * tok, W), BF),
             pltpu.VMEM((2 * C, rows, W), BF),
@@ -338,9 +392,6 @@
             pltpu.VMEM((rows, Z * tok), BF),
             pltpu.VMEM((Z, 16, tok), F32),
             pltpu.VMEM((rows, 1), F32),
-            pltpu.VMEM((C, W, FE), BF),
-            pltpu.VMEM((C, W, FE), BF),
-            pltpu.VMEM((C, FE, W), BF),
             pltpu.VMEM((rows, FE), F32),
             pltpu.VMEM((rows, FE), F32),
             pltpu.VMEM((rows, FE), F32),
@@ -349,24 +400,24 @@
             pltpu.VMEM((rows, FE), BF),
             pltpu.VMEM((C, rows, W), BF),
             pltpu.VMEM((C, Z - 1, tok, W), BF),
+            pltpu.VMEM((C, tok, W), BF),
             dma((Z,)), dma((Z,)),
             dma((2 * C, Z - 1, 2)), dma((2 * C, Z - 1, 2)),
             dma((2 * C,)), dma((2 * C,)),
             dma((C,)), dma((C,)),
             dma((C, Z)), dma((C, Z)),
-            dma((2 * C,)), dma((3,)), dma((3, C)),
+            dma((C,)), dma((2 * C,)), dma((3,)),
         ],
         compiler_params=pltpu.CompilerParams(
-            collective_id=0, has_side_effects=True, vmem_limit_bytes=63 * 1024 * 1024),
+            collective_id=0, has_side_effects=True, vmem_limit_bytes=50 * 1024 * 1024),
         cost_estimate=pl.CostEstimate(
             flops=16 * rows * width * FE, bytes_accessed=12 * width * FE, transcendentals=rows * FE),
     )(
         info, tokens, grad_out,
         w_gate[0].reshape(C, W, FE), w_up[0].reshape(C, W, FE), w_down[0],
     )
-    grad_tokens = jnp.transpose(gt, (1, 0, 2)).reshape(tok, width)
     return (
-        grad_tokens,
+        gt,
         wgo.reshape(1, width, FE),
         wuo.reshape(1, width, FE),
         wdo[None],

time: 216 us -> 195 us (0.903)
  the two profiles are of different devices: /device:TPU:11 before, /device:TPU:0 now
where the time goes in v2:
time: 195 us
  Pallas kernels  186 us (95%)
  local copies, waits for them, and re-layouts  6.61 us (3%)
  other arithmetic  1.98 us (1%)
    pallas_call x1, Pallas kernels, local(): pl.pallas_call(functools.partial(kernel, sizes), out_shape=(pltpu.VMEM((t...  186 us
    unnamed x4, local copies, waits for them, and re-layouts  6.61 us

profile of v2, /device:TPU:0, one launch (start us, length us, event | category | flops | bytes accessed | tf_op | source)
XLA Modules:
  0.0 194.9 jit_solution(18396454355491896068)
XLA Ops:
  0.6 0.7 convert_bitcast_fusion
  1.3 1.3 select_maximum_fusion.info
  2.6 185.7 %shard_map.102 = (bf16[128,2560]{1,0:T(8,128)(2,1)S(1)}, bf16[10,256,768]{2,1,0:T(8,128)(2,1)S(1)}, bf16[10,256,768]{2,1,0:T(8,128)(2,1)S(1)}, bf16[768,2560]{1,0:T(8,128)(2,1)S(1)}) custom-call(f32[16,128]{1,0:T(8,128)} %select_maximum_fusion.info, bf16[128,2560]{1,0:T(8,128)(2,1)} %tokens.1, bf16[128,2560]{1,0:T(8,128)(2,1)} %grad.1, ...), custom_call_target="tpu_custom_call" | custom-call | flops 28185722880 | bytes 23592960 | tf_op jit(solution)/shard_map/pallas_call | solution.py:378
  188.3 0.8 copy.15
  189.1 1.9 copy.16
  191.0 1.9 copy.17
  193.0 1.9 copy.18

commit v3 on v2

--- a/solution.py
+++ b/solution.py
@@ -18,7 +18,7 @@
 
 def kernel(
     sizes,
-    info, tokens, grad, wg, wu, wd,
+    ids, gates, tokens, grad, wg, wu, wd,
     gt, wgv, wuv, wdv,
     xall, snd, rcv, mm, infog, scale, gp, up, ag, act, gg, ug, rrv, zrv, rly,
     info_send, info_recv, ag_send, ag_recv, pl_send, pl_recv, rt_send, rt_recv, zr_send, zr_recv,
@@ -52,10 +52,8 @@
         load = pltpu.make_async_copy(src, own(z, i), x_sem.at[i])
         load.start()
         loads.append(load)
-    pltpu.make_async_copy(wg, wgv, w_sem.at[0]).start()
-    pltpu.make_async_copy(wu, wuv, w_sem.at[1]).start()
-    pltpu.make_async_copy(wd, wdv, w_sem.at[2]).start()
-    infog[z] = info[...]
+    infog[z, 0:top, :] = ids[...].astype(F32)
+    infog[z, 8:8 + top, :] = gates[...]
 
     barrier = pltpu.get_barrier_semaphore()
 
@@ -206,13 +204,24 @@
             def _(h):
                 ag[half_rows(h), :] = dot(rcv[k, half_rows(h), :], wdv[:, cols(k - C)], 1, 1)
 
-        @pl.when(k > C)
+        @pl.when((k > C) & (k < 2 * C - 1))
         def _():
             @pl.loop(0, 2)
             def _(h):
                 ag[half_rows(h), :] += dot(rcv[k, half_rows(h), :], wdv[:, cols(k - C)], 1, 1)
 
-    @pl.loop(0, 2 * C + Z)
+        @pl.when(k == 2 * C - 1)
+        def _():
+            @pl.loop(0, 2)
+            def _(h):
+                part = half_rows(h)
+                grad_act = ag[part, :] + dot(rcv[k, part, :], wdv[:, cols(k - C)], 1, 1)
+                gg[part, :] = (grad_act * gp[part, :]).astype(BF)
+                ug[part, :] = (grad_act * up[part, :]).astype(BF)
+
+    lag = 1 + Z
+
+    @pl.loop(0, 2 * C + lag)
     def _(i):
         for step in range(Z):
             j = i - step
@@ -231,25 +240,20 @@
 
         @pl.when(i == 0)
         def _():
+            pltpu.make_async_copy(wg, wgv, w_sem.at[0]).start()
+            pltpu.make_async_copy(wu, wuv, w_sem.at[1]).start()
+            pltpu.make_async_copy(wd, wdv, w_sem.at[2]).start()
             routing()
 
         @pl.when((i >= Z - 1) & (i < 2 * C + Z - 1))
         def _():
             gather(i - (Z - 1))
 
-        @pl.when(i >= Z)
-        def _():
-            consume(i - Z)
-
-    @pl.loop(0, rows // 32)
-    def _(h):
-        part = pl.ds(pl.multiple_of(h * 32, 32), 32)
-        gg[part, :] = (ag[part, :] * gp[part, :]).astype(BF)
-        ug[part, :] = (ag[part, :] * up[part, :]).astype(BF)
-
-    @pl.loop(0, 2 * C)
-    def _(j):
-        wait_bytes(snd.at[j, others], pl_send.at[j])
+        @pl.when(i >= lag)
+        def _():
+            consume(i - lag)
+
+    def line_sent(j):
         for step in range(Z - 1):
             for way in range(2):
                 @pl.when(ag_sends(step, way))
@@ -258,6 +262,8 @@
 
     @pl.loop(0, C)
     def _(c):
+        wait_bytes(snd.at[c, others], pl_send.at[c])
+
         @pl.loop(0, 2)
         def _(h):
             snd[c, half_rows(h), :] = (
@@ -333,6 +339,9 @@
             wgv[c] = dot(rcv[c], gg[...], 0, 0).astype(BF)
             wuv[c] = dot(rcv[c], ug[...], 0, 0).astype(BF)
             wdv[:, cols(c)] = dot(act[...], rcv[c + C], 0, 0).astype(BF)
+            line_sent(c)
+            line_sent(c + C)
+            wait_bytes(snd.at[c + C, others], pl_send.at[c + C])
             wait_bytes(rrv.at[c, others], rt_recv.at[c])
             xall[c] = dot(mm[...], rrv[c], 0, 0).astype(BF)
             send_partials(c)
@@ -344,12 +353,9 @@
         @pl.when(c > 1)
         def _():
             finish(c - 2)
-
-    @pl.loop(0, C)
-    def _(c):
-        wait_bytes(snd.at[c, others], rt_send.at[c])
-        for d in range(1, Z):
-            line_copy(c, d).wait_send()
+            wait_bytes(snd.at[c - 2, others], rt_send.at[c - 2])
+            for d in range(1, Z):
+                line_copy(c - 2, d).wait_send()
 
 
 def local(tokens, grad_out, expert_ids, gate_weights, w_gate, w_up, w_down):
@@ -368,10 +374,6 @@
     C = width // W
     rows = NP * R
     sizes = (Z, inner, NP, S, cap, R, top, tok, C, W, FE)
-    info = jnp.concatenate([
-        jnp.pad(expert_ids.T.astype(F32), ((0, 8 - top), (0, 0))),
-        jnp.pad(gate_weights.T, ((0, 8 - top), (0, 0))),
-    ])
     any_spec = pl.BlockSpec(memory_space=pl.ANY)
     vmem_spec = pl.BlockSpec(memory_space=pltpu.VMEM)
     dma = pltpu.SemaphoreType.DMA
@@ -383,7 +385,7 @@
             pltpu.VMEM((C, W, FE), BF),
             pltpu.VMEM((FE, width), BF),
         ),
-        in_specs=[vmem_spec] + [any_spec] * 5,
+        in_specs=[vmem_spec] * 2 + [any_spec] * 5,
         out_specs=(vmem_spec,) * 4,
         scratch_shapes=[
             pltpu.VMEM((2 * C, Z * tok, W), BF),
@@ -413,7 +415,7 @@
         cost_estimate=pl.CostEstimate(
             flops=16 * rows * width * FE, bytes_accessed=12 * width * FE, transcendentals=rows * FE),
     )(
-        info, tokens, grad_out,
+        expert_ids.T, gate_weights.T, tokens, grad_out,
         w_gate[0].reshape(C, W, FE), w_up[0].reshape(C, W, FE), w_down[0],
     )
     return (

time: 195 us -> 192 us (0.985)
  Pallas kernels: 186 us -> 184 us
  other arithmetic: 1.98 us -> 0 us
where the time goes in v3:
time: 192 us
  Pallas kernels  184 us (96%)
  local copies, waits for them, and re-layouts  6.61 us (3%)
    pallas_call x1, Pallas kernels, local(): pl.pallas_call(functools.partial(kernel, sizes), out_shape=(pltpu.VMEM((t...  184 us
    unnamed x4, local copies, waits for them, and re-layouts  6.61 us

profile of v3, /device:TPU:0, one launch (start us, length us, event | category | flops | bytes accessed | tf_op | source)
XLA Modules:
  0.0 191.7 jit_solution(12295130131440665687)
XLA Ops:
  0.6 184.4 %shard_map.102 = (bf16[128,2560]{1,0:T(8,128)(2,1)S(1)}, bf16[10,256,768]{2,1,0:T(8,128)(2,1)S(1)}, bf16[10,256,768]{2,1,0:T(8,128)(2,1)S(1)}, bf16[768,2560]{1,0:T(8,128)(2,1)S(1)}) custom-call(s32[6,128]{1,0:T(8,128)} %bitcast.14, f32[6,128]{1,0:T(8,128)} %bitcast.15, bf16[128,2560]{1,0:T(8,128)(2,1)} %tokens.1, bf16[128,2560]{1,0:T(8,128)(2,1)} %grad.1, ...), custom_call_target="tpu_custom_call" | custom-call | flops 28185722880 | bytes 23592960 | tf_op jit(solution)/shard_map/pallas_call | solution.py:380
  185.1 0.8 copy.15
  185.9 1.9 %copy.16 = bf16[1,2560,768]{2,1,0:T(8,128)(2,1)} copy(bf16[1,2560,768]{2,1,0:T(8,128)(2,1)S(1)} %bitcast.10) | data formatting | bytes 7864320
  187.8 1.9 %copy.17 = bf16[1,2560,768]{2,1,0:T(8,128)(2,1)} copy(bf16[1,2560,768]{2,1,0:T(8,128)(2,1)S(1)} %bitcast.9) | data formatting | bytes 7864320
  189.8 1.9 %copy.18 = bf16[1,768,2560]{2,1,0:T(8,128)(2,1)} copy(bf16[1,768,2560]{2,1,0:T(8,128)(2,1)S(1)} %bitcast.8) | data formatting | bytes 7864320
